TPU v7x, 512 devices: a whole 4x4x16 slice. The times are simulated.
512 devices in a mesh: grp: 32 (over x, z_hi, core), leaf: 16 (over y, z_lo).
Axes of the slice: x: 4, y: 4, z: 16 (z_hi: 4, z_lo: 4; z = z_hi * 4 + z_lo), core: 2. Of those that a mesh axis runs over, the one named last changes fastest.
Arguments:
- charges: bfloat16 [64, 524288], P(None, ('grp', 'leaf')), may hold values from -6 to 6
- interp_basis: bfloat16 [2048, 256, 128], P(('grp', 'leaf')), may hold values from -0.375 to 0.375
- coupling: bfloat16 [4, 2048, 2, 128, 128], P(None, ('grp', 'leaf')), may hold values from -0.5 to 0.5
- expand_basis: bfloat16 [2048, 128, 256], P(('grp', 'leaf')), may hold values from -0.5 to 0.5
- block_rank: int32 [5, 2048], P(None, ('grp', 'leaf')), may hold values from 64 to 128
- leaf_partner: int32 [2048], P(('grp', 'leaf')), may hold values from 0 to 2047, as said below
Outputs:
- potential: bfloat16 [64, 524288], P(None, ('grp', 'leaf'))
Inputs may be any that keep to these rules, and one draw needn't show every extreme that they name: leaf_partner is a permutation of the blocks that maps every aligned run of 64 blocks onto itself.
All inputs are finite; a program needn't handle non-finite values.
Results may differ from a plain program's by a relative error of at most 0.0075.
Values may be sent and summed in bfloat16 or wider, within the bound.
A program may use at most 64 MiB of HBM per device.

v0:
```python
import jax
import jax.numpy as jnp
from jax import lax
from jax.sharding import PartitionSpec as P

LEVELS = 3


def swapped(shard, axis, distance):
    return lax.ppermute(shard, axis, [(i, i ^ 1 << distance) for i in range(lax.axis_size(axis))])


def masked(values, ranks):
    cols = jnp.arange(values.shape[-1], dtype=jnp.int32)
    keep = (cols[None, None, :] < ranks[:, None, None]).astype(jnp.float32)
    return values * keep


def apply_pair(own, other, factors, ranks):
    first = jnp.einsum("brk,bkq->brq", own, factors[:, 0], preferred_element_type=jnp.float32)
    second = jnp.einsum("brk,bkq->brq", other, factors[:, 1], preferred_element_type=jnp.float32)
    return masked(first + second, ranks).astype(jnp.bfloat16)


def shards(charges, interp_basis, coupling, expand_basis, block_rank, leaf_partner):
    local_blocks = interp_basis.shape[0]
    size_m = interp_basis.shape[1]
    rhs_count = charges.shape[0]
    grouped = charges.reshape(rhs_count, local_blocks, size_m)
    compressed = jnp.einsum(
        "rbm,bmk->brk", grouped, interp_basis, preferred_element_type=jnp.float32
    )
    compressed = masked(compressed, block_rank[0]).astype(jnp.bfloat16)
    leaf_count = lax.axis_size("leaf")
    group_size = local_blocks * leaf_count
    group_start = lax.axis_index("grp") * group_size
    wanted = leaf_partner - group_start
    subtree = lax.all_gather(compressed, "leaf", axis=0, tiled=True)
    picked = subtree[wanted]
    state = apply_pair(compressed, picked, coupling[0], block_rank[1])
    grp_bits = lax.axis_size("grp").bit_length() - 1
    for level in range(LEVELS):
        bit = (level + 1) * grp_bits // LEVELS - 1
        other = swapped(state, "grp", bit)
        state = apply_pair(state, other, coupling[level + 1], block_rank[level + 2])
    result = jnp.einsum("brk,bkm->rbm", state, expand_basis, preferred_element_type=jnp.float32)
    return result.reshape(rhs_count, local_blocks * size_m).astype(jnp.bfloat16)


def solution(mesh):
    in_specs = (
        P(None, ("grp", "leaf")),
        P(("grp", "leaf"), None, None),
        P(None, ("grp", "leaf"), None, None, None),
        P(("grp", "leaf"), None, None),
        P(None, ("grp", "leaf")),
        P(("grp", "leaf")),
    )
    out_specs = P(None, ("grp", "leaf"))
    return jax.shard_map(shards, mesh=mesh, in_specs=in_specs, out_specs=out_specs, check_vma=False)
```

profile of v0, /device:TPU:1, one launch (start us, length us, event | category | flops | bytes accessed | tf_op | source)
XLA Modules:
  0.0 138.4 jit_solution(4260829388127726227)
XLA Ops:
  6.5 0.0 copy-start
  6.5 0.0 all-gather.2.cloned.1.call-start
  6.5 1.1 slice_reduce_fusion
  7.7 0.1 fusion.17
  7.7 1.8 %fusion.9 = bf16[4,64,128]{2,1,0:T(8,128)(2,1)} fusion(bf16[4,256,128]{2,1,0:T(8,128)(2,1)} %param.7, bf16[8,4,8,256]{3,2,1,0:T(8,128)(2,1)} %bitcast.63, f32[4,128]{1,0:T(4,128)S(1)} %fusion.17), kind=kOutput, calls=%fused_computation.16 | convolution fusion | flops 16842752 | bytes 460800 | tf_op jit(solution)/shard_map/rbm,bmk->brk/dot_general | solution.py:30
  9.6 0.0 all-gather.2.cloned.1.call-update
  9.6 1.3 fusion.22
  11.0 0.0 copy-start.1
  11.0 0.0 copy-start.2
  11.0 0.6 copy-done.2
  11.7 0.1 fusion.21
  11.8 0.1 fusion.19
  11.8 0.1 fusion.18
  11.9 0.1 fusion.20
  12.0 0.0 copy-done.1
  12.0 0.2 fusion.15
  12.1 80.8 %all-gather.2.cloned.1.call-done = bf16[64,64,128]{2,1,0:T(8,128)(2,1)} async-done(((bf16[4,64,128]{2,1,0:T(8,128)(2,1)}), bf16[64,64,128]{2,1,0:T(8,128)(2,1)}) %all-gather.2.cloned.1.call-update) | async-done | bytes 1048592 | tf_op jit(solution)/shard_map/all_gather | solution.py:38
  93.0 1.8 %gather_fusion = bf16[4,64,128]{2,1,0:T(8,128)(2,1)S(1)} fusion(bf16[64,64,128]{2,1,0:T(8,128)(2,1)} %all-gather.2.cloned.1.call-done, s32[1024]{0:T(1024)S(1)} %pad_clamp_fusion), kind=kCustom, calls=%fused_computation | custom fusion | bytes 131088 | tf_op jit(solution)/shard_map/gather | solution.py:39
  94.8 0.2 fusion.8
  94.9 12.2 %collective-permute-start = (bf16[4,64,128]{2,1,0:T(8,128)(2,1)S(1)}, bf16[4,64,128]{2,1,0:T(8,128)(2,1)S(1)}, u32[]{:S(2)}, u32[]{:S(2)}) collective-permute-start(bf16[4,64,128]{2,1,0:T(8,128)(2,1)S(1)} %fusion.8), channel_id=1, source_target_pairs={{0,16},{16,0},{32,48},{48,32},{64,80},{80,64},{96,112},{112,96},{1... | collective-permute-start | bytes 196616 | tf_op jit(solution)/shard_map/ppermute | solution.py:10
  107.2 0.2 fusion.14
  107.3 0.7 collective-permute-done
  108.1 0.2 fusion.7
  108.2 11.8 %collective-permute-start.1 = (bf16[4,64,128]{2,1,0:T(8,128)(2,1)S(1)}, bf16[4,64,128]{2,1,0:T(8,128)(2,1)S(1)}, u32[]{:S(2)}, u32[]{:S(2)}) collective-permute-start(bf16[4,64,128]{2,1,0:T(8,128)(2,1)S(1)} %fusion.7), channel_id=1, source_target_pairs={{0,64},{16,80},{32,96},{48,112},{64,0},{80,16},{96,32},{112,48},{1... | collective-permute-start | bytes 196616 | tf_op jit(solution)/shard_map/ppermute | solution.py:10
  120.0 0.1 fusion.13
  120.2 3.7 %collective-permute-done.1 = bf16[4,64,128]{2,1,0:T(8,128)(2,1)S(1)} collective-permute-done((bf16[4,64,128]{2,1,0:T(8,128)(2,1)S(1)}, bf16[4,64,128]{2,1,0:T(8,128)(2,1)S(1)}, u32[]{:S(2)}, u32[]{:S(2)}) %collective-permute-start.1) | collective-permute-done | bytes 65568 | tf_op jit(solution)/shard_map/ppermute | solution.py:10
  123.9 0.2 fusion.6
  124.1 4.2 %collective-permute-start.2 = (bf16[4,64,128]{2,1,0:T(8,128)(2,1)S(1)}, bf16[4,64,128]{2,1,0:T(8,128)(2,1)S(1)}, u32[]{:S(2)}, u32[]{:S(2)}) collective-permute-start(bf16[4,64,128]{2,1,0:T(8,128)(2,1)S(1)} %fusion.6), channel_id=1, source_target_pairs={{0,256},{16,272},{32,288},{48,304},{64,320},{80,336},{96,352},{112... | collective-permute-start | bytes 196616 | tf_op jit(solution)/shard_map/ppermute | solution.py:10
  128.3 0.1 fusion.12
  128.4 2.2 %collective-permute-done.2 = bf16[4,64,128]{2,1,0:T(8,128)(2,1)S(1)} collective-permute-done((bf16[4,64,128]{2,1,0:T(8,128)(2,1)S(1)}, bf16[4,64,128]{2,1,0:T(8,128)(2,1)S(1)}, u32[]{:S(2)}, u32[]{:S(2)}) %collective-permute-start.2) | collective-permute-done | bytes 65568 | tf_op jit(solution)/shard_map/ppermute | solution.py:10
  130.6 0.0 copy-done
  130.6 0.3 fusion
  130.9 0.7 copy.27
  (6 shorter events, 0.1 us)
Async XLA Ops:
  6.5 124.1 %copy-start = (bf16[4,128,256]{2,1,0:T(8,128)(2,1)S(1)}, bf16[4,128,256]{2,1,0:T(8,128)(2,1)}, u32[]{:S(2)}) copy-start(bf16[4,128,256]{2,1,0:T(8,128)(2,1)} %param.9) | copy-start | bytes 786436
  6.5 86.4 %all-gather.2.cloned.1.call-start = ((), (), s32[]{:S(2)}) async-start(), calls=%async_computation | async-start | bytes 1114112 | tf_op jit(solution)/shard_map/all_gather | solution.py:38
  11.0 1.0 copy-start.1
  11.0 0.7 copy-start.2
  94.9 13.1 %collective-permute-start = (bf16[4,64,128]{2,1,0:T(8,128)(2,1)S(1)}, bf16[4,64,128]{2,1,0:T(8,128)(2,1)S(1)}, u32[]{:S(2)}, u32[]{:S(2)}) collective-permute-start(bf16[4,64,128]{2,1,0:T(8,128)(2,1)S(1)} %fusion.8), channel_id=1, source_target_pairs={{0,16},{16,0},{32,48},{48,32},{64,80},{80,64},{96,112},{112,96},{1... | collective-permute-start | bytes 196616 | tf_op jit(solution)/shard_map/ppermute | solution.py:10
  108.2 15.7 %collective-permute-start.1 = (bf16[4,64,128]{2,1,0:T(8,128)(2,1)S(1)}, bf16[4,64,128]{2,1,0:T(8,128)(2,1)S(1)}, u32[]{:S(2)}, u32[]{:S(2)}) collective-permute-start(bf16[4,64,128]{2,1,0:T(8,128)(2,1)S(1)} %fusion.7), channel_id=1, source_target_pairs={{0,64},{16,80},{32,96},{48,112},{64,0},{80,16},{96,32},{112,48},{1... | collective-permute-start | bytes 196616 | tf_op jit(solution)/shard_map/ppermute | solution.py:10
  124.1 6.5 %collective-permute-start.2 = (bf16[4,64,128]{2,1,0:T(8,128)(2,1)S(1)}, bf16[4,64,128]{2,1,0:T(8,128)(2,1)S(1)}, u32[]{:S(2)}, u32[]{:S(2)}) collective-permute-start(bf16[4,64,128]{2,1,0:T(8,128)(2,1)S(1)} %fusion.6), channel_id=1, source_target_pairs={{0,256},{16,272},{32,288},{48,304},{64,320},{80,336},{96,352},{112... | collective-permute-start | bytes 196616 | tf_op jit(solution)/shard_map/ppermute | solution.py:10
Sparse Core Ops, SparseCore 0:
  9.7 83.2 all-gather.1
where the time goes:
time: 139 us; the launch traced here: 138 us
  waiting for transfers between devices  87.5 us (63%)
  starting transfers between devices  28.2 us (20%)
  between operations  13.5 us (10%)
  local copies, waits for them, and re-layouts  5.59 us (4%)
  matrix products  3.22 us (2%)
    all_gather x1, waiting for transfers between devices, shards(): subtree = lax.all_gather(compressed, 'leaf', axis=0, tiled=True)  80.8 us
    ppermute x3, starting transfers between devices, swapped(): lax.ppermute(shard, axis, [(i, i ^ 1 << distance) for i in range(lax.axis...  28.2 us
    ppermute x3, waiting for transfers between devices, swapped(): lax.ppermute(shard, axis, [(i, i ^ 1 << distance) for i in range(lax.axis...  6.61 us
  transfers between devices with their start and end apart: 4, of which 4 were waited for; matrix products, arithmetic and copies ran while one was open for 2% of the time, Pallas kernels for 0%

commit v1 on v0

v1 whole, which is shorter than its diff:
```python
import jax
import jax.numpy as jnp
from jax import lax
from jax.experimental import pallas as pl
from jax.experimental.pallas import tpu as pltpu
from jax.sharding import PartitionSpec as P

LEVELS = 3
MESH = pl.DeviceIdType.MESH


def kernel(
    charges_hbm, interp_hbm, coupling_hbm, expand_hbm, rank_ref, partner_ref, out_hbm,
    charges, interp, coupling, expand, out, subtree, state, other,
    load_sems, gather_send, gather_recv, level_send, level_recv, out_sems,
):
    grp, leaf = lax.axis_index("grp"), lax.axis_index("leaf")
    n_leaf = lax.axis_size("leaf")
    grp_bits = lax.axis_size("grp").bit_length() - 1
    blocks, size_m, rank = interp.shape
    rows = charges.shape[0]

    mates = [lax.rem(leaf + step, n_leaf) for step in range(1, n_leaf)]
    pairs = []
    for level in range(LEVELS):
        stride = 1 << ((level + 1) * grp_bits // LEVELS - 1)
        pairs.append(grp + stride * (1 - 2 * lax.rem(grp // stride, 2)))
    barrier = pltpu.get_barrier_semaphore()
    for pair in pairs:
        pl.semaphore_signal(barrier, inc=1, device_id=(pair, leaf), device_id_type=MESH)
    for mate in mates:
        pl.semaphore_signal(barrier, inc=1, device_id=(grp, mate), device_id_type=MESH)

    loads = [
        pltpu.make_async_copy(src, dst, load_sems.at[i])
        for i, (src, dst) in enumerate(
            ((charges_hbm, charges), (interp_hbm, interp), (coupling_hbm, coupling), (expand_hbm, expand))
        )
    ]
    for load in loads:
        load.start()

    cols = lax.broadcasted_iota(jnp.int32, (rows, rank), 1)

    def keep(section, block, values):
        return jnp.where(cols < rank_ref[section, block], values, 0.0).astype(jnp.bfloat16)

    def dot(a, b):
        return jnp.dot(a, b, preferred_element_type=jnp.float32)

    loads[0].wait()
    loads[1].wait()
    for block in range(blocks):
        made = dot(charges[:, pl.ds(block * size_m, size_m)], interp[block])
        subtree[leaf * blocks + block] = keep(0, block, made)

    pl.semaphore_wait(barrier, len(mates) + len(pairs))
    mine = subtree.at[pl.ds(leaf * blocks, blocks)]
    sends = []
    for step, mate in enumerate(mates):
        send = pltpu.make_async_remote_copy(
            src_ref=mine, dst_ref=mine, send_sem=gather_send.at[step], recv_sem=gather_recv.at[step],
            device_id=(grp, mate), device_id_type=MESH,
        )
        send.start()
        sends.append(send)

    loads[2].wait()
    own = [dot(subtree[leaf * blocks + block], coupling[0, block, 0]) for block in range(blocks)]
    for send in sends:
        send.wait_recv()
    for block in range(blocks):
        picked = subtree[lax.rem(partner_ref[block], blocks * n_leaf)]
        state[0, block] = keep(1, block, own[block] + dot(picked, coupling[0, block, 1]))

    for level in range(LEVELS):
        swap = pltpu.make_async_remote_copy(
            src_ref=state.at[level], dst_ref=other.at[level],
            send_sem=level_send.at[level], recv_sem=level_recv.at[level],
            device_id=(pairs[level], leaf), device_id_type=MESH,
        )
        swap.start()
        sends.append(swap)
        own = [dot(state[level, block], coupling[level + 1, block, 0]) for block in range(blocks)]
        swap.wait_recv()
        for block in range(blocks):
            total = own[block] + dot(other[level, block], coupling[level + 1, block, 1])
            state[level + 1, block] = keep(level + 2, block, total)

    loads[3].wait()
    stores = []
    for block in range(blocks):
        part = pl.ds(block * size_m, size_m)
        out[:, part] = dot(state[LEVELS, block], expand[block]).astype(jnp.bfloat16)
        store = pltpu.make_async_copy(out.at[:, part], out_hbm.at[:, part], out_sems.at[block])
        store.start()
        stores.append(store)
    for send in sends:
        send.wait_send()
    for store in stores:
        store.wait()


def shards(charges, interp_basis, coupling, expand_basis, block_rank, leaf_partner):
    n_leaf = lax.axis_size("leaf")
    blocks, size_m, rank = interp_basis.shape
    rows = charges.shape[0]
    any_spec = pl.BlockSpec(memory_space=pl.ANY)
    smem_spec = pl.BlockSpec(memory_space=pltpu.SMEM)
    bf16 = jnp.bfloat16
    return pl.pallas_call(
        kernel,
        out_shape=jax.ShapeDtypeStruct(charges.shape, bf16),
        in_specs=[any_spec] * 4 + [smem_spec] * 2,
        out_specs=any_spec,
        scratch_shapes=[
            pltpu.VMEM(charges.shape, bf16),
            pltpu.VMEM(interp_basis.shape, bf16),
            pltpu.VMEM(coupling.shape, bf16),
            pltpu.VMEM(expand_basis.shape, bf16),
            pltpu.VMEM(charges.shape, bf16),
            pltpu.VMEM((n_leaf * blocks, rows, rank), bf16),
            pltpu.VMEM((LEVELS + 1, blocks, rows, rank), bf16),
            pltpu.VMEM((LEVELS, blocks, rows, rank), bf16),
            pltpu.SemaphoreType.DMA((4,)),
            pltpu.SemaphoreType.DMA((n_leaf - 1,)),
            pltpu.SemaphoreType.DMA((n_leaf - 1,)),
            pltpu.SemaphoreType.DMA((LEVELS,)),
            pltpu.SemaphoreType.DMA((LEVELS,)),
            pltpu.SemaphoreType.DMA((blocks,)),
        ],
        compiler_params=pltpu.CompilerParams(
            collective_id=0, has_side_effects=True, vmem_limit_bytes=60 * 1024 * 1024
        ),
    )(charges, interp_basis, coupling, expand_basis, block_rank, leaf_partner)


def solution(mesh):
    in_specs = (
        P(None, ("grp", "leaf")),
        P(("grp", "leaf"), None, None),
        P(None, ("grp", "leaf"), None, None, None),
        P(("grp", "leaf"), None, None),
        P(None, ("grp", "leaf")),
        P(("grp", "leaf")),
    )
    out_specs = P(None, ("grp", "leaf"))
    return jax.shard_map(shards, mesh=mesh, in_specs=in_specs, out_specs=out_specs, check_vma=False)
```

time: 139 us -> 57.2 us (0.41)
  waiting for transfers between devices: 87.5 us -> 0 us
  Pallas kernels: 0 us -> 54.1 us
  starting transfers between devices: 28.2 us -> 0 us
  between operations: 13.5 us -> 0.01 us
  matrix products: 3.22 us -> 0 us
  local copies, waits for them, and re-layouts: 5.59 us -> 2.92 us
    all_gather x1 -> x0, waiting for transfers between devices: 80.8 us -> none  [shards(): subtree = lax.all_gather(compressed, 'leaf', axis=0, tiled=True)]
    pallas_call x0 -> x1, Pallas kernels: none -> 54.1 us  [shards(): pl.pallas_call(kernel, out_shape=jax.ShapeDtypeStruct(charges.shape, bf16...]
    ppermute x3 -> x0, starting transfers between devices: 28.2 us -> none  [swapped(): lax.ppermute(shard, axis, [(i, i ^ 1 << distance) for i in range(lax.axis...]
    ppermute x3 -> x0, waiting for transfers between devices: 6.61 us -> none  [swapped(): lax.ppermute(shard, axis, [(i, i ^ 1 << distance) for i in range(lax.axis...]
    dot_general x9 -> x0, matrix products: 3.22 us -> none  [the longest x1 1.84 us: shards(): jnp.einsum('rbm,bmk->brk', grouped, interp_basis, preferred_element_type=...]
    slice x2 -> x0, local copies, waits for them, and re-layouts: 2.41 us -> none  [shards(): state = apply_pair(state, other, coupling[level + 1], block_rank[level + 2])]
    unnamed x10 -> x2, local copies, waits for them, and re-layouts: 0.73 us -> 2.92 us
    gather x1 -> x0, local copies, waits for them, and re-layouts: 1.79 us -> none  [shards(): picked = subtree[wanted]]
  transfers between devices with their start and end apart: 4 -> 0, of which waited for: 4 -> 0; matrix products, arithmetic and copies ran while one was open for 2% -> 0% of each run, Pallas kernels for 0% -> 0%
where the time goes in v1:
time: 57.2 us; the launch traced here: 57 us
  Pallas kernels  54.1 us (95%)
  local copies, waits for them, and re-layouts  2.92 us (5%)
    pallas_call x1, Pallas kernels, shards(): pl.pallas_call(kernel, out_shape=jax.ShapeDtypeStruct(charges.shape, bf16...  54.1 us
    unnamed x2, local copies, waits for them, and re-layouts  2.92 us

profile of v1, /device:TPU:1, one launch (start us, length us, event | category | flops | bytes accessed | tf_op | source)
XLA Modules:
  0.0 57.0 jit_solution(6622098189489686589)
XLA Ops:
  0.0 1.4 %copy.7.rank_ref = s32[5,4]{1,0:T(8,128)} copy(s32[5,4]{0,1:T(4,128)} %param.10) | data formatting | bytes 160 | tf_op args[4]
  1.4 54.1 %shard_map.64 = bf16[64,1024]{1,0:T(8,128)(2,1)} custom-call(bf16[64,1024]{1,0:T(8,128)(2,1)} %charges_hbm.1, bf16[4,256,128]{2,1,0:T(8,128)(2,1)} %interp_hbm.1, bf16[4,4,2,128,128]{4,3,2,1,0:T(8,128)(2,1)} %coupling_hbm.1, bf16[4,128,256]{2,1,0:T(8,128)(2,1)} %expand_hbm.1, s32[5,4]{1,0:T(8,128)} %copy.7.rank_ref, s32[4]{0:T(128)} %partner_ref.1), custom_call_target="tpu_custom_call" | custom-call | tf_op jit(solution)/shard_map/pallas_call | solution.py:111
  55.4 1.6 %copy.9 = bf16[64,1024]{1,0:T(8,128)(2,1)} copy(bf16[64,1024]{1,0:T(8,128)(2,1)} %shard_map.64) | data formatting | bytes 262144

commit v2 on v1

v2 whole, which is shorter than its diff:
```python
import math

import jax
import jax.numpy as jnp
from jax import lax
from jax.experimental import pallas as pl
from jax.experimental.pallas import tpu as pltpu
from jax.sharding import PartitionSpec as P

LEVELS = 3
MESH = pl.DeviceIdType.MESH


def kernel(
    charges_hbm, interp_hbm, coupling_hbm, expand_hbm, rank_ref, partner_ref, out_hbm,
    charges, interp, coupling, expand, out, wanted, near_y, near_z, picked, found_z, found_y, state, other,
    load_sems, ask_send, ask_recv, near_send, near_recv, far_send, far_recv,
    level_send, level_recv, out_sems,
):
    grp, leaf = lax.axis_index("grp"), lax.axis_index("leaf")
    n_leaf = lax.axis_size("leaf")
    near, found = (near_y, near_z), (found_z, found_y)
    side = near_y.shape[0]
    grp_bits = lax.axis_size("grp").bit_length() - 1
    blocks, size_m, rank = interp.shape
    rows = charges.shape[0]
    half = rows // 2

    place = (leaf // side, lax.rem(leaf, side))

    def peer(axis, step):
        at = lax.rem(place[axis] + step, side)
        return at, (at * side + place[1] if axis == 0 else place[0] * side + at)

    pairs = []
    for level in range(LEVELS):
        stride = 1 << ((level + 1) * grp_bits // LEVELS - 1)
        pairs.append(grp + stride * (1 - 2 * lax.rem(grp // stride, 2)))
    barrier = pltpu.get_barrier_semaphore()
    for pair in pairs:
        pl.semaphore_signal(barrier, inc=1, device_id=(pair, leaf), device_id_type=MESH)
    for axis in range(2):
        for step in range(1, side):
            pl.semaphore_signal(
                barrier, inc=1, device_id=(grp, peer(axis, step)[1]), device_id_type=MESH
            )

    loads = [
        pltpu.make_async_copy(src, dst, load_sems.at[i])
        for i, (src, dst) in enumerate(
            ((charges_hbm, charges), (interp_hbm, interp), (coupling_hbm, coupling), (expand_hbm, expand))
        )
    ]
    for load in loads:
        load.start()

    def remote(src, dst, send_sem, recv_sem, device):
        return pltpu.make_async_remote_copy(
            src_ref=src, dst_ref=dst, send_sem=send_sem, recv_sem=recv_sem,
            device_id=device, device_id_type=MESH,
        )

    cols = lax.broadcasted_iota(jnp.int32, (rows, rank), 1)

    def keep(section, block, values):
        mask = cols[: values.shape[0]] < rank_ref[block, section]
        return jnp.where(mask, values, 0.0).astype(jnp.bfloat16)

    def dot(a, b):
        return jnp.dot(a, b, preferred_element_type=jnp.float32)

    loads[0].wait()
    loads[1].wait()
    leaves = []
    for block in range(blocks):
        made = keep(0, block, dot(charges[:, pl.ds(block * size_m, size_m)], interp[block]))
        leaves.append(made)
        for h in range(2):
            near[h][place[h], block] = made[h * half : (h + 1) * half]

    pl.semaphore_wait(barrier, 2 * (side - 1) + LEVELS)
    asks, nears, fars = [], [], []
    for h in range(2):
        for step in range(1, side):
            k = h * (side - 1) + step - 1
            first, second = peer(h, step), peer(1 - h, step)
            ask = remote(
                partner_ref, wanted.at[h, place[1 - h]], ask_send.at[k], ask_recv.at[k], (grp, second[1])
            )
            ask.start()
            asks.append(ask)
            mine = near[h].at[place[h]]
            send = remote(mine, mine, near_send.at[k], near_recv.at[k], (grp, first[1]))
            send.start()
            nears.append(send)

    loads[2].wait()
    own = [dot(leaves[block], coupling[0, block, 0]) for block in range(blocks)]
    for ask in asks:
        ask.wait_recv()

    def origin(value):
        at = lax.rem(value, blocks * n_leaf)
        device, block = at // blocks, lax.rem(at, blocks)
        return (device // side, lax.rem(device, side)), block

    for h in range(2):
        for step in range(1, side):
            nears[h * (side - 1) + step - 1].wait_recv()
        for step in range(1, side):
            k = h * (side - 1) + step - 1
            at, device = peer(1 - h, step)
            for block in range(blocks):
                source, index = origin(wanted[h, at, block])
                picked[h, step - 1, block] = near[h][source[h], index]
            send = remote(
                picked.at[h, step - 1], found[h].at[place[1 - h]], far_send.at[k], far_recv.at[k], (grp, device)
            )
            send.start()
            fars.append(send)
        for block in range(blocks):
            source, index = origin(partner_ref[block])
            found[h][place[1 - h], block] = near[h][source[h], index]
    for far in fars:
        far.wait_recv()
    for block in range(blocks):
        source, _ = origin(partner_ref[block])
        for h in range(2):
            total = dot(found[h][source[1 - h], block], coupling[0, block, 1])
            part = slice(h * half, (h + 1) * half)
            state[0, block, part] = keep(1, block, own[block][part] + total)

    sends = asks + nears + fars
    for level in range(LEVELS):
        swap = remote(
            state.at[level], other.at[level], level_send.at[level], level_recv.at[level], (pairs[level], leaf)
        )
        swap.start()
        sends.append(swap)
        own = [dot(state[level, block], coupling[level + 1, block, 0]) for block in range(blocks)]
        swap.wait_recv()
        for block in range(blocks):
            total = own[block] + dot(other[level, block], coupling[level + 1, block, 1])
            state[level + 1, block] = keep(level + 2, block, total)

    loads[3].wait()
    stores = []
    for block in range(blocks):
        part = pl.ds(block * size_m, size_m)
        out[:, part] = dot(state[LEVELS, block], expand[block]).astype(jnp.bfloat16)
        store = pltpu.make_async_copy(out.at[:, part], out_hbm.at[:, part], out_sems.at[block])
        store.start()
        stores.append(store)
    for send in sends:
        send.wait_send()
    for store in stores:
        store.wait()


def shards(charges, interp_basis, coupling, expand_basis, block_rank, leaf_partner):
    side = math.isqrt(lax.axis_size("leaf"))
    blocks, size_m, rank = interp_basis.shape
    rows = charges.shape[0]
    any_spec = pl.BlockSpec(memory_space=pl.ANY)
    smem_spec = pl.BlockSpec(memory_space=pltpu.SMEM)
    bf16 = jnp.bfloat16
    return pl.pallas_call(
        kernel,
        out_shape=jax.ShapeDtypeStruct(charges.shape, bf16),
        in_specs=[any_spec] * 4 + [smem_spec] * 2,
        out_specs=any_spec,
        scratch_shapes=[
            pltpu.VMEM(charges.shape, bf16),
            pltpu.VMEM(interp_basis.shape, bf16),
            pltpu.VMEM(coupling.shape, bf16),
            pltpu.VMEM(expand_basis.shape, bf16),
            pltpu.VMEM(charges.shape, bf16),
            pltpu.SMEM((2, side, blocks), jnp.int32),
            *[pltpu.VMEM((side, blocks, rows // 2, rank), bf16)] * 2,
            pltpu.VMEM((2, side - 1, blocks, rows // 2, rank), bf16),
            *[pltpu.VMEM((side, blocks, rows // 2, rank), bf16)] * 2,
            pltpu.VMEM((LEVELS + 1, blocks, rows, rank), bf16),
            pltpu.VMEM((LEVELS, blocks, rows, rank), bf16),
            pltpu.SemaphoreType.DMA((4,)),
            *[pltpu.SemaphoreType.DMA((2 * (side - 1),))] * 6,
            pltpu.SemaphoreType.DMA((LEVELS,)),
            pltpu.SemaphoreType.DMA((LEVELS,)),
            pltpu.SemaphoreType.DMA((blocks,)),
        ],
        compiler_params=pltpu.CompilerParams(
            collective_id=0, has_side_effects=True, vmem_limit_bytes=60 * 1024 * 1024
        ),
    )(charges, interp_basis, coupling, expand_basis, block_rank.T, leaf_partner)


def solution(mesh):
    in_specs = (
        P(None, ("grp", "leaf")),
        P(("grp", "leaf"), None, None),
        P(None, ("grp", "leaf"), None, None, None),
        P(("grp", "leaf"), None, None),
        P(None, ("grp", "leaf")),
        P(("grp", "leaf")),
    )
    out_specs = P(None, ("grp", "leaf"))
    return jax.shard_map(shards, mesh=mesh, in_specs=in_specs, out_specs=out_specs, check_vma=False)
```

time: 57.2 us -> 40.6 us (0.71)
  Pallas kernels: 54.1 us -> 38.3 us
  local copies, waits for them, and re-layouts: 2.92 us -> 1.57 us
    pallas_call x1, Pallas kernels: 54.1 us -> 38.3 us  [shards(): pl.pallas_call(kernel, out_shape=jax.ShapeDtypeStruct(charges.shape, bf16...]
    unnamed x2 -> x1, local copies, waits for them, and re-layouts: 2.92 us -> 1.57 us
where the time goes in v2:
time: 40.6 us; the launch traced here: 39.9 us
  Pallas kernels  38.3 us (94%)
  local copies, waits for them, and re-layouts  1.57 us (4%)
    pallas_call x1, Pallas kernels, shards(): pl.pallas_call(kernel, out_shape=jax.ShapeDtypeStruct(charges.shape, bf16...  38.3 us
    unnamed x1, local copies, waits for them, and re-layouts  1.57 us

profile of v2, /device:TPU:1, one launch (start us, length us, event | category | flops | bytes accessed | tf_op | source)
XLA Modules:
  0.0 39.9 jit_solution(8609578063969955824)
XLA Ops:
  0.0 38.3 %shard_map.64 = bf16[64,1024]{1,0:T(8,128)(2,1)} custom-call(bf16[64,1024]{1,0:T(8,128)(2,1)} %charges_hbm.1, bf16[4,256,128]{2,1,0:T(8,128)(2,1)} %interp_hbm.1, bf16[4,4,2,128,128]{4,3,2,1,0:T(8,128)(2,1)} %coupling_hbm.1, bf16[4,128,256]{2,1,0:T(8,128)(2,1)} %expand_hbm.1, s32[4,5]{1,0:T(4,128)} %bitcast.1, s32[4]{0:T(128)} %partner_ref.1), custom_call_target="tpu_custom_call" | custom-call | tf_op jit(solution)/shard_map/pallas_call | solution.py:167
  38.3 1.6 %copy.8 = bf16[64,1024]{1,0:T(8,128)(2,1)} copy(bf16[64,1024]{1,0:T(8,128)(2,1)} %shard_map.64) | data formatting | bytes 262144

commit v3 on v2

v3 whole, which is shorter than its diff:
```python
import math

import jax
import jax.numpy as jnp
from jax import lax
from jax.experimental import pallas as pl
from jax.experimental.pallas import tpu as pltpu
from jax.sharding import PartitionSpec as P

LEVELS = 3
PARTS = 2
MESH = pl.DeviceIdType.MESH


def dot(a, b):
    return jnp.dot(a, b, preferred_element_type=jnp.float32)


def kernel(
    charges_hbm, interp_hbm, coupling_hbm, expand_hbm, rank_ref, partner_ref, out,
    charges, interp, coupling, expand, wanted, picked, state, other,
    load_sems, ask_send, ask_recv, near_send, near_recv, far_send, far_recv,
    level_send, level_recv, answer, *gathered,
):
    near, found = gathered[:PARTS], gathered[PARTS:]
    grp, leaf = lax.axis_index("grp"), lax.axis_index("leaf")
    n_leaf = lax.axis_size("leaf")
    side = near[0].shape[0]
    grp_bits = lax.axis_size("grp").bit_length() - 1
    blocks, size_m, rank = interp.shape
    rows = charges.shape[0]
    part = rows // PARTS

    place = (leaf // side, lax.rem(leaf, side))

    def peer(axis, step):
        at = lax.rem(place[axis] + step, side)
        return at, (at * side + place[1] if axis == 0 else place[0] * side + at)

    pairs, strides = [], []
    for level in range(LEVELS):
        stride = 1 << ((level + 1) * grp_bits // LEVELS - 1)
        strides.append(stride)
        pairs.append(grp + stride * (1 - 2 * lax.rem(grp // stride, 2)))
    barrier = pltpu.get_barrier_semaphore()
    upper = lax.rem(grp // strides[1], 2)

    def greet(pair):
        pl.semaphore_signal(barrier, inc=1, device_id=(pair, leaf), device_id_type=MESH)

    greet(pairs[0])
    greet(pairs[2])
    pl.when(upper == 0)(lambda: greet(pairs[1]))
    for axis in range(2):
        for step in range(1, side):
            pl.semaphore_signal(
                barrier, inc=1, device_id=(grp, peer(axis, step)[1]), device_id_type=MESH
            )

    loads = [
        pltpu.make_async_copy(src, dst, load_sems.at[i])
        for i, (src, dst) in enumerate(
            ((charges_hbm, charges), (interp_hbm, interp), (coupling_hbm, coupling), (expand_hbm, expand))
        )
    ]
    loads[0].start()
    loads[1].start()

    def remote(src, dst, send_sem, recv_sem, device):
        return pltpu.make_async_remote_copy(
            src_ref=src, dst_ref=dst, send_sem=send_sem, recv_sem=recv_sem,
            device_id=device, device_id_type=MESH,
        )

    cols = lax.broadcasted_iota(jnp.int32, (rows, rank), 1)

    def keep(section, block, values):
        mask = cols[: values.shape[0]] < rank_ref[block, section]
        return jnp.where(mask, values, 0.0).astype(jnp.bfloat16)

    loads[0].wait()
    loads[1].wait()
    loads[2].start()
    loads[3].start()
    leaves = []
    for block in range(blocks):
        made = keep(0, block, dot(charges[:, pl.ds(block * size_m, size_m)], interp[block]))
        leaves.append(made)
        for q in range(PARTS):
            near[q][place[q % 2], block] = made[q * part : (q + 1) * part]

    pl.semaphore_wait(barrier, 2 * (side - 1) + LEVELS - 1 + upper)

    @pl.when(upper == 1)
    def _():
        pl.semaphore_signal(answer, inc=1, device_id=(pairs[1], leaf), device_id_type=MESH)

    asks = []
    for axis in range(2):
        for step in range(1, side):
            k = axis * (side - 1) + step - 1
            ask = remote(
                partner_ref, wanted.at[axis, place[axis]], ask_send.at[k], ask_recv.at[k],
                (grp, peer(axis, step)[1]),
            )
            ask.start()
            asks.append(ask)
    nears = [[] for _ in range(PARTS)]
    for q in range(PARTS):
        for step in range(1, side):
            mine = near[q].at[place[q % 2]]
            send = remote(
                mine, mine, near_send.at[q, step - 1], near_recv.at[q, step - 1],
                (grp, peer(q % 2, step)[1]),
            )
            send.start()
            nears[q].append(send)

    loads[2].wait()
    whole = [dot(leaves[block], coupling[0, block, 0]) for block in range(blocks)]
    for ask in asks:
        ask.wait_recv()

    def origin(value):
        at = lax.bitwise_and(value, blocks * n_leaf - 1)
        device, block = lax.shift_right_logical(at, blocks.bit_length() - 1), lax.bitwise_and(at, blocks - 1)
        z_bits = side.bit_length() - 1
        return (lax.shift_right_logical(device, z_bits), lax.bitwise_and(device, side - 1)), block

    sources = [origin(partner_ref[block]) for block in range(blocks)]
    asked = [
        [[origin(wanted[axis, peer(axis, step)[0], block]) for block in range(blocks)] for step in range(1, side)]
        for axis in range(2)
    ]

    fars = [[] for _ in range(PARTS)]
    swaps = [[None] * PARTS for _ in range(LEVELS)]
    owns = [[None] * PARTS for _ in range(LEVELS)]

    def pick(q):
        first, second = q % 2, 1 - q % 2
        for send in nears[q]:
            send.wait_recv()
        for step in range(1, side):
            device = peer(second, step)[1]
            for block in range(blocks):
                source, index = asked[second][step - 1][block]
                picked[q, step - 1, block] = near[q][source[first], index]
            send = remote(
                picked.at[q, step - 1], found[q].at[place[second]],
                far_send.at[q, step - 1], far_recv.at[q, step - 1], (grp, device),
            )
            send.start()
            fars[q].append(send)
        for block in range(blocks):
            source, index = sources[block]
            found[q][place[second], block] = near[q][source[first], index]

    def send_level(level, q):
        swap = remote(
            state.at[level, q], other.at[level, q], level_send.at[level, q], level_recv.at[level, q],
            (pairs[level], leaf),
        )
        swap.start()
        swaps[level][q] = swap

    def own_level(level, q):
        owns[level][q] = [
            dot(state[level, q, block], coupling[level + 1, block, 0]) for block in range(blocks)
        ]

    def leaf_step(q):
        for send in fars[q]:
            send.wait_recv()
        for block in range(blocks):
            source, _ = sources[block]
            total = dot(found[q][source[1 - q % 2], block], coupling[0, block, 1])
            state[0, q, block] = keep(1, block, whole[block][q * part : (q + 1) * part] + total)
        send_level(0, q)
        own_level(0, q)

    def level_step(level, q):
        swaps[level][q].wait_recv()
        for block in range(blocks):
            total = owns[level][q][block] + dot(other[level, q, block], coupling[level + 1, block, 1])
            state[level + 1, q, block] = keep(level + 2, block, total)
        if level + 1 < LEVELS:
            send_level(level + 1, q)
            own_level(level + 1, q)

    def expand_step(q):
        here = pl.ds(q * part, part)
        for block in range(blocks):
            out[here, pl.ds(block * size_m, size_m)] = dot(state[LEVELS, q, block], expand[block]).astype(
                jnp.bfloat16
            )

    for q in range(PARTS):
        pick(q)
    for q in range(PARTS + 1):
        if q < PARTS:
            leaf_step(q)
        if q == 1:
            pl.when(upper == 0)(lambda: pl.semaphore_wait(answer, 1))
        if q >= 1:
            level_step(0, q - 1)
    loads[3].wait()
    for send in asks + sum(nears + fars, []) + swaps[0]:
        send.wait_send()
    lag = PARTS // 2
    for q in range(PARTS + lag):
        if q < PARTS:
            level_step(1, q)
        if q >= lag:
            level_step(2, q - lag)
            expand_step(q - lag)
    for send in swaps[1] + swaps[2]:
        send.wait_send()


def shards(charges, interp_basis, coupling, expand_basis, block_rank, leaf_partner):
    side = math.isqrt(lax.axis_size("leaf"))
    blocks, size_m, rank = interp_basis.shape
    rows = charges.shape[0]
    part = rows // PARTS
    any_spec = pl.BlockSpec(memory_space=pltpu.HBM)
    smem_spec = pl.BlockSpec(memory_space=pltpu.SMEM)
    bf16 = jnp.bfloat16
    dma = pltpu.SemaphoreType.DMA
    return pl.pallas_call(
        kernel,
        out_shape=pltpu.VMEM(charges.shape, bf16),
        in_specs=[any_spec] * 4 + [smem_spec] * 2,
        out_specs=pl.BlockSpec(memory_space=pltpu.VMEM),
        scratch_shapes=[
            pltpu.VMEM(charges.shape, bf16),
            pltpu.VMEM(interp_basis.shape, bf16),
            pltpu.VMEM(coupling.shape, bf16),
            pltpu.VMEM(expand_basis.shape, bf16),
            pltpu.SMEM((2, side, blocks), jnp.int32),
            pltpu.VMEM((PARTS, side - 1, blocks, part, rank), bf16),
            pltpu.VMEM((LEVELS + 1, PARTS, blocks, part, rank), bf16),
            pltpu.VMEM((LEVELS, PARTS, blocks, part, rank), bf16),
            dma((4,)),
            *[dma((2 * (side - 1),))] * 2,
            *[dma((PARTS, side - 1))] * 4,
            *[dma((LEVELS, PARTS))] * 2,
            pltpu.SemaphoreType.REGULAR,
            *[pltpu.VMEM((side, blocks, part, rank), bf16)] * (2 * PARTS),
        ],
        compiler_params=pltpu.CompilerParams(
            collective_id=0, has_side_effects=True, vmem_limit_bytes=60 * 1024 * 1024
        ),
    )(charges, interp_basis, coupling, expand_basis, block_rank.T, leaf_partner)


def solution(mesh):
    in_specs = (
        P(None, ("grp", "leaf")),
        P(("grp", "leaf"), None, None),
        P(None, ("grp", "leaf"), None, None, None),
        P(("grp", "leaf"), None, None),
        P(None, ("grp", "leaf")),
        P(("grp", "leaf")),
    )
    out_specs = P(None, ("grp", "leaf"))
    return jax.shard_map(shards, mesh=mesh, in_specs=in_specs, out_specs=out_specs, check_vma=False)
```

time: 40.6 us -> 38.8 us (0.956)
  local copies, waits for them, and re-layouts: 1.57 us -> 0.66 us
  Pallas kernels: 38.3 us -> 37.4 us
    pallas_call x1, Pallas kernels: 38.3 us -> 37.4 us  [shards(): pl.pallas_call(kernel, out_shape=pltpu.VMEM(charges.shape, bf16), in_spec...]
    unnamed x1, local copies, waits for them, and re-layouts: 1.57 us -> 0.66 us
where the time goes in v3:
time: 38.8 us; the launch traced here: 38.1 us
  Pallas kernels  37.4 us (96%)
  local copies, waits for them, and re-layouts  0.66 us (2%)
    pallas_call x1, Pallas kernels, shards(): pl.pallas_call(kernel, out_shape=pltpu.VMEM(charges.shape, bf16), in_spec...  37.4 us

profile of v3, /device:TPU:1, one launch (start us, length us, event | category | flops | bytes accessed | tf_op | source)
XLA Modules:
  0.0 38.1 jit_solution(13551854055502518319)
XLA Ops:
  0.0 37.4 %shard_map.64 = bf16[64,1024]{1,0:T(8,128)(2,1)S(1)} custom-call(bf16[64,1024]{1,0:T(8,128)(2,1)} %charges_hbm.1, bf16[4,256,128]{2,1,0:T(8,128)(2,1)} %interp_hbm.1, bf16[4,4,2,128,128]{4,3,2,1,0:T(8,128)(2,1)} %coupling_hbm.1, bf16[4,128,256]{2,1,0:T(8,128)(2,1)} %expand_hbm.1, s32[4,5]{1,0:T(4,128)} %bitcast.1, s32[4]{0:T(128)} %partner_ref.1), custom_call_target="tpu_custom_call" | custom-call | tf_op jit(solution)/shard_map/pallas_call | solution.py:230
  37.4 0.7 %copy.8 = bf16[64,1024]{1,0:T(8,128)(2,1)} copy(bf16[64,1024]{1,0:T(8,128)(2,1)S(1)} %shard_map.64) | data formatting | bytes 262144

commit v4 on v3

--- a/solution.py
+++ b/solution.py
@@ -17,8 +17,8 @@
 
 
 def kernel(
-    charges_hbm, interp_hbm, coupling_hbm, expand_hbm, rank_ref, partner_ref, out,
-    charges, interp, coupling, expand, wanted, picked, state, other,
+    charges_hbm, interp_hbm, coupling_hbm, expand_hbm, rank_hbm, partner_hbm, out,
+    charges, interp, coupling, expand, rank_ref, partner_ref, wanted, picked, state, other,
     load_sems, ask_send, ask_recv, near_send, near_recv, far_send, far_recv,
     level_send, level_recv, answer, *gathered,
 ):
@@ -60,11 +60,14 @@
     loads = [
         pltpu.make_async_copy(src, dst, load_sems.at[i])
         for i, (src, dst) in enumerate(
-            ((charges_hbm, charges), (interp_hbm, interp), (coupling_hbm, coupling), (expand_hbm, expand))
+            (
+                (charges_hbm, charges), (interp_hbm, interp), (coupling_hbm, coupling), (expand_hbm, expand),
+                (rank_hbm, rank_ref), (partner_hbm, partner_ref),
+            )
         )
     ]
-    loads[0].start()
-    loads[1].start()
+    for i in (4, 5, 0, 1):
+        loads[i].start()
 
     def remote(src, dst, send_sem, recv_sem, device):
         return pltpu.make_async_remote_copy(
@@ -78,8 +81,8 @@
         mask = cols[: values.shape[0]] < rank_ref[block, section]
         return jnp.where(mask, values, 0.0).astype(jnp.bfloat16)
 
-    loads[0].wait()
-    loads[1].wait()
+    for i in (4, 5, 0, 1):
+        loads[i].wait()
     loads[2].start()
     loads[3].start()
     leaves = []
@@ -223,25 +226,26 @@
     blocks, size_m, rank = interp_basis.shape
     rows = charges.shape[0]
     part = rows // PARTS
-    any_spec = pl.BlockSpec(memory_space=pltpu.HBM)
-    smem_spec = pl.BlockSpec(memory_space=pltpu.SMEM)
+    hbm_spec = pl.BlockSpec(memory_space=pltpu.HBM)
     bf16 = jnp.bfloat16
     dma = pltpu.SemaphoreType.DMA
     return pl.pallas_call(
         kernel,
         out_shape=pltpu.VMEM(charges.shape, bf16),
-        in_specs=[any_spec] * 4 + [smem_spec] * 2,
+        in_specs=[hbm_spec] * 6,
         out_specs=pl.BlockSpec(memory_space=pltpu.VMEM),
         scratch_shapes=[
             pltpu.VMEM(charges.shape, bf16),
             pltpu.VMEM(interp_basis.shape, bf16),
             pltpu.VMEM(coupling.shape, bf16),
             pltpu.VMEM(expand_basis.shape, bf16),
+            pltpu.SMEM(block_rank.shape[::-1], jnp.int32),
+            pltpu.SMEM(leaf_partner.shape, jnp.int32),
             pltpu.SMEM((2, side, blocks), jnp.int32),
             pltpu.VMEM((PARTS, side - 1, blocks, part, rank), bf16),
             pltpu.VMEM((LEVELS + 1, PARTS, blocks, part, rank), bf16),
             pltpu.VMEM((LEVELS, PARTS, blocks, part, rank), bf16),
-            dma((4,)),
+            dma((6,)),
             *[dma((2 * (side - 1),))] * 2,
             *[dma((PARTS, side - 1))] * 4,
             *[dma((LEVELS, PARTS))] * 2,

time: 38.8 us -> 38.1 us (0.982)
  Pallas kernels: 37.4 us -> 36.7 us
    pallas_call x1, Pallas kernels: 37.4 us -> 36.7 us  [shards(): pl.pallas_call(kernel, out_shape=pltpu.VMEM(charges.shape, bf16), in_spec...]
where the time goes in v4:
time: 38.1 us; the launch traced here: 37.4 us
  Pallas kernels  36.7 us (96%)
  local copies, waits for them, and re-layouts  0.66 us (2%)
    pallas_call x1, Pallas kernels, shards(): pl.pallas_call(kernel, out_shape=pltpu.VMEM(charges.shape, bf16), in_spec...  36.7 us

profile of v4, /device:TPU:1, one launch (start us, length us, event | category | flops | bytes accessed | tf_op | source)
XLA Modules:
  0.0 37.4 jit_solution(4256266966013174787)
XLA Ops:
  0.0 36.7 %shard_map.64 = bf16[64,1024]{1,0:T(8,128)(2,1)S(1)} custom-call(bf16[64,1024]{1,0:T(8,128)(2,1)} %charges_hbm.1, bf16[4,256,128]{2,1,0:T(8,128)(2,1)} %interp_hbm.1, bf16[4,4,2,128,128]{4,3,2,1,0:T(8,128)(2,1)} %coupling_hbm.1, bf16[4,128,256]{2,1,0:T(8,128)(2,1)} %expand_hbm.1, s32[4,5]{1,0:T(4,128)} %bitcast.1, s32[4]{0:T(128)} %partner_hbm.1), custom_call_target="tpu_custom_call" | custom-call | tf_op jit(solution)/shard_map/pallas_call | solution.py:232
  36.7 0.7 %copy.8 = bf16[64,1024]{1,0:T(8,128)(2,1)} copy(bf16[64,1024]{1,0:T(8,128)(2,1)S(1)} %shard_map.64) | data formatting | bytes 262144

commit v5 on v4

--- a/solution.py
+++ b/solution.py
@@ -155,9 +155,6 @@
             )
             send.start()
             fars[q].append(send)
-        for block in range(blocks):
-            source, index = sources[block]
-            found[q][place[second], block] = near[q][source[first], index]
 
     def send_level(level, q):
         swap = remote(
@@ -180,7 +177,6 @@
             total = dot(found[q][source[1 - q % 2], block], coupling[0, block, 1])
             state[0, q, block] = keep(1, block, whole[block][q * part : (q + 1) * part] + total)
         send_level(0, q)
-        own_level(0, q)
 
     def level_step(level, q):
         swaps[level][q].wait_recv()
@@ -189,7 +185,6 @@
             state[level + 1, q, block] = keep(level + 2, block, total)
         if level + 1 < LEVELS:
             send_level(level + 1, q)
-            own_level(level + 1, q)
 
     def expand_step(q):
         here = pl.ds(q * part, part)
@@ -200,23 +195,29 @@
 
     for q in range(PARTS):
         pick(q)
-    for q in range(PARTS + 1):
-        if q < PARTS:
-            leaf_step(q)
-        if q == 1:
-            pl.when(upper == 0)(lambda: pl.semaphore_wait(answer, 1))
-        if q >= 1:
-            level_step(0, q - 1)
+    for q in range(PARTS):
+        for block in range(blocks):
+            source, index = sources[block]
+            found[q][place[1 - q % 2], block] = near[q][source[q % 2], index]
+    for q in range(PARTS):
+        leaf_step(q)
+    for q in range(PARTS):
+        own_level(0, q)
+    pl.when(upper == 0)(lambda: pl.semaphore_wait(answer, 1))
+    for q in range(PARTS):
+        level_step(0, q)
+    for q in range(PARTS):
+        own_level(1, q)
     loads[3].wait()
     for send in asks + sum(nears + fars, []) + swaps[0]:
         send.wait_send()
-    lag = PARTS // 2
-    for q in range(PARTS + lag):
-        if q < PARTS:
-            level_step(1, q)
-        if q >= lag:
-            level_step(2, q - lag)
-            expand_step(q - lag)
+    for q in range(PARTS):
+        level_step(1, q)
+    for q in range(PARTS):
+        own_level(2, q)
+    for q in range(PARTS):
+        level_step(2, q)
+        expand_step(q)
     for send in swaps[1] + swaps[2]:
         send.wait_send()
 

time: 38.1 us -> 38.1 us (level)
  no operation moved by 1% of the time
where the time goes in v5:
time: 38.1 us; the launch traced here: 37.4 us
  Pallas kernels  36.7 us (96%)
  local copies, waits for them, and re-layouts  0.66 us (2%)
    pallas_call x1, Pallas kernels, shards(): pl.pallas_call(kernel, out_shape=pltpu.VMEM(charges.shape, bf16), in_spec...  36.7 us

profile of v5, /device:TPU:1, one launch (start us, length us, event | category | flops | bytes accessed | tf_op | source)
XLA Modules:
  0.0 37.4 jit_solution(2311597549339912206)
XLA Ops:
  0.0 36.7 %shard_map.64 = bf16[64,1024]{1,0:T(8,128)(2,1)S(1)} custom-call(bf16[64,1024]{1,0:T(8,128)(2,1)} %charges_hbm.1, bf16[4,256,128]{2,1,0:T(8,128)(2,1)} %interp_hbm.1, bf16[4,4,2,128,128]{4,3,2,1,0:T(8,128)(2,1)} %coupling_hbm.1, bf16[4,128,256]{2,1,0:T(8,128)(2,1)} %expand_hbm.1, s32[4,5]{1,0:T(4,128)} %bitcast.1, s32[4]{0:T(128)} %partner_hbm.1), custom_call_target="tpu_custom_call" | custom-call | tf_op jit(solution)/shard_map/pallas_call | solution.py:233
  36.7 0.7 %copy.8 = bf16[64,1024]{1,0:T(8,128)(2,1)} copy(bf16[64,1024]{1,0:T(8,128)(2,1)S(1)} %shard_map.64) | data formatting | bytes 262144

commit v6 on v5

--- a/solution.py
+++ b/solution.py
@@ -94,10 +94,6 @@
 
     pl.semaphore_wait(barrier, 2 * (side - 1) + LEVELS - 1 + upper)
 
-    @pl.when(upper == 1)
-    def _():
-        pl.semaphore_signal(answer, inc=1, device_id=(pairs[1], leaf), device_id_type=MESH)
-
     asks = []
     for axis in range(2):
         for step in range(1, side):
@@ -195,12 +191,20 @@
 
     for q in range(PARTS):
         pick(q)
+    @pl.when(jnp.logical_and(upper == 1, lax.rem(place[1], 2) == 1))
+    def _():
+        pl.semaphore_signal(answer, inc=1, device_id=(pairs[1], leaf), device_id_type=MESH)
+
     for q in range(PARTS):
         for block in range(blocks):
             source, index = sources[block]
             found[q][place[1 - q % 2], block] = near[q][source[q % 2], index]
     for q in range(PARTS):
         leaf_step(q)
+    @pl.when(jnp.logical_and(upper == 1, lax.rem(place[1], 2) == 0))
+    def _():
+        pl.semaphore_signal(answer, inc=1, device_id=(pairs[1], leaf), device_id_type=MESH)
+
     for q in range(PARTS):
         own_level(0, q)
     pl.when(upper == 0)(lambda: pl.semaphore_wait(answer, 1))

time: 38.1 us -> 37 us (0.971); the launches traced: 37.4 us -> 36.9 us
  Pallas kernels: 36.7 us -> 36.2 us
    pallas_call x1, Pallas kernels: 36.7 us -> 36.2 us  [shards(): pl.pallas_call(kernel, out_shape=pltpu.VMEM(charges.shape, bf16), in_spec...]
where the time goes in v6:
time: 37 us; the launch traced here: 36.9 us
  Pallas kernels  36.2 us (98%)
  local copies, waits for them, and re-layouts  0.66 us (2%)
    pallas_call x1, Pallas kernels, shards(): pl.pallas_call(kernel, out_shape=pltpu.VMEM(charges.shape, bf16), in_spec...  36.2 us

profile of v6, /device:TPU:1, one launch (start us, length us, event | category | flops | bytes accessed | tf_op | source)
XLA Modules:
  0.0 36.9 jit_solution(17988205095021380743)
XLA Ops:
  0.0 36.2 %shard_map.64 = bf16[64,1024]{1,0:T(8,128)(2,1)S(1)} custom-call(bf16[64,1024]{1,0:T(8,128)(2,1)} %charges_hbm.1, bf16[4,256,128]{2,1,0:T(8,128)(2,1)} %interp_hbm.1, bf16[4,4,2,128,128]{4,3,2,1,0:T(8,128)(2,1)} %coupling_hbm.1, bf16[4,128,256]{2,1,0:T(8,128)(2,1)} %expand_hbm.1, s32[4,5]{1,0:T(4,128)} %bitcast.1, s32[4]{0:T(128)} %partner_hbm.1), custom_call_target="tpu_custom_call" | custom-call | tf_op jit(solution)/shard_map/pallas_call | solution.py:237
  36.2 0.7 %copy.8 = bf16[64,1024]{1,0:T(8,128)(2,1)} copy(bf16[64,1024]{1,0:T(8,128)(2,1)S(1)} %shard_map.64) | data formatting | bytes 262144

commit v7 on v6

--- a/solution.py
+++ b/solution.py
@@ -20,7 +20,7 @@
     charges_hbm, interp_hbm, coupling_hbm, expand_hbm, rank_hbm, partner_hbm, out,
     charges, interp, coupling, expand, rank_ref, partner_ref, wanted, picked, state, other,
     load_sems, ask_send, ask_recv, near_send, near_recv, far_send, far_recv,
-    level_send, level_recv, answer, *gathered,
+    level_send, level_recv, answer, folded, *gathered,
 ):
     near, found = gathered[:PARTS], gathered[PARTS:]
     grp, leaf = lax.axis_index("grp"), lax.axis_index("leaf")
@@ -105,8 +105,8 @@
             ask.start()
             asks.append(ask)
     nears = [[] for _ in range(PARTS)]
-    for q in range(PARTS):
-        for step in range(1, side):
+    for step in range(1, side):
+        for q in range(PARTS):
             mine = near[q].at[place[q % 2]]
             send = remote(
                 mine, mine, near_send.at[q, step - 1], near_recv.at[q, step - 1],
@@ -179,15 +179,17 @@
         for block in range(blocks):
             total = owns[level][q][block] + dot(other[level, q, block], coupling[level + 1, block, 1])
             state[level + 1, q, block] = keep(level + 2, block, total)
-        if level + 1 < LEVELS:
-            send_level(level + 1, q)
-
-    def expand_step(q):
+        send_level(level + 1, q)
+
+    def own_last(q):
+        owns[LEVELS - 1][q] = [dot(state[LEVELS - 1, q, block], folded[0, block]) for block in range(blocks)]
+
+    def last_step(q):
         here = pl.ds(q * part, part)
-        for block in range(blocks):
-            out[here, pl.ds(block * size_m, size_m)] = dot(state[LEVELS, q, block], expand[block]).astype(
-                jnp.bfloat16
-            )
+        swaps[LEVELS - 1][q].wait_recv()
+        for block in range(blocks):
+            total = owns[LEVELS - 1][q][block] + dot(other[LEVELS - 1, q, block], folded[1, block])
+            out[here, pl.ds(block * size_m, size_m)] = total.astype(jnp.bfloat16)
 
     for q in range(PARTS):
         pick(q)
@@ -199,6 +201,14 @@
         for block in range(blocks):
             source, index = sources[block]
             found[q][place[1 - q % 2], block] = near[q][source[q % 2], index]
+    loads[3].wait()
+    width = lax.broadcasted_iota(jnp.int32, (rank, rank), 1)
+    for side_of in range(2):
+        for block in range(blocks):
+            kept = jnp.where(
+                width < rank_ref[block, LEVELS + 1], coupling[LEVELS, block, side_of].astype(jnp.float32), 0.0
+            ).astype(jnp.bfloat16)
+            folded[side_of, block] = dot(kept, expand[block]).astype(jnp.bfloat16)
     for q in range(PARTS):
         leaf_step(q)
     @pl.when(jnp.logical_and(upper == 1, lax.rem(place[1], 2) == 0))
@@ -212,16 +222,14 @@
         level_step(0, q)
     for q in range(PARTS):
         own_level(1, q)
-    loads[3].wait()
     for send in asks + sum(nears + fars, []) + swaps[0]:
         send.wait_send()
     for q in range(PARTS):
         level_step(1, q)
     for q in range(PARTS):
-        own_level(2, q)
-    for q in range(PARTS):
-        level_step(2, q)
-        expand_step(q)
+        own_last(q)
+    for q in range(PARTS):
+        last_step(q)
     for send in swaps[1] + swaps[2]:
         send.wait_send()
 
@@ -248,13 +256,14 @@
             pltpu.SMEM(leaf_partner.shape, jnp.int32),
             pltpu.SMEM((2, side, blocks), jnp.int32),
             pltpu.VMEM((PARTS, side - 1, blocks, part, rank), bf16),
-            pltpu.VMEM((LEVELS + 1, PARTS, blocks, part, rank), bf16),
+            pltpu.VMEM((LEVELS, PARTS, blocks, part, rank), bf16),
             pltpu.VMEM((LEVELS, PARTS, blocks, part, rank), bf16),
             dma((6,)),
             *[dma((2 * (side - 1),))] * 2,
             *[dma((PARTS, side - 1))] * 4,
             *[dma((LEVELS, PARTS))] * 2,
             pltpu.SemaphoreType.REGULAR,
+            pltpu.VMEM((2, blocks, rank, size_m), bf16),
             *[pltpu.VMEM((side, blocks, part, rank), bf16)] * (2 * PARTS),
         ],
         compiler_params=pltpu.CompilerParams(

time: 37 us -> 36.9 us (level)
  no operation moved by 1% of the time
where the time goes in v7:
time: 36.9 us; the launch traced here: 36.7 us
  Pallas kernels  36.1 us (98%)
  local copies, waits for them, and re-layouts  0.66 us (2%)
    pallas_call x1, Pallas kernels, shards(): pl.pallas_call(kernel, out_shape=pltpu.VMEM(charges.shape, bf16), in_spec...  36.1 us

profile of v7, /device:TPU:1, one launch (start us, length us, event | category | flops | bytes accessed | tf_op | source)
XLA Modules:
  0.0 36.7 jit_solution(7508200064461507238)
XLA Ops:
  0.0 36.1 %shard_map.64 = bf16[64,1024]{1,0:T(8,128)(2,1)S(1)} custom-call(bf16[64,1024]{1,0:T(8,128)(2,1)} %charges_hbm.1, bf16[4,256,128]{2,1,0:T(8,128)(2,1)} %interp_hbm.1, bf16[4,4,2,128,128]{4,3,2,1,0:T(8,128)(2,1)} %coupling_hbm.1, bf16[4,128,256]{2,1,0:T(8,128)(2,1)} %expand_hbm.1, s32[4,5]{1,0:T(4,128)} %bitcast.1, s32[4]{0:T(128)} %partner_hbm.1), custom_call_target="tpu_custom_call" | custom-call | tf_op jit(solution)/shard_map/pallas_call | solution.py:245
  36.1 0.7 %copy.8 = bf16[64,1024]{1,0:T(8,128)(2,1)} copy(bf16[64,1024]{1,0:T(8,128)(2,1)S(1)} %shard_map.64) | data formatting | bytes 262144
